TPU v7x, 32 devices: a whole 2x2x4 slice. The times are simulated.
32 devices in a mesh: dp: 4 (over z), seq: 2 (over x), mp: 4 (over y, core).
Axes of the slice: x: 2, y: 2, z: 4, core: 2. Of those that a mesh axis runs over, the one named last changes fastest.
Arguments:
- queries: bfloat16 [4, 2, 4, 64, 4096], P('dp', 'seq', None, None, 'mp'), may hold values from -8 to 8
- key_vectors: bfloat16 [4, 2, 4, 64, 4096], P('dp', 'seq', None, None, 'mp'), may hold values from -8 to 8
- value_rows: bfloat16 [4, 2, 4, 64, 4096], P('dp', 'seq', None, None, 'mp'), may hold values from -6 to 6
- upstream: bfloat16 [4, 2, 4, 64, 4096], P('dp', 'seq', None, None, 'mp'), may hold values from -6 to 6
- segments: int32 [4, 512], P('dp'), may hold values from 0 to 7, never falling along the last dimension, each value on 1 to 128 neighbouring positions
- losses: float32 [4, 8], P('dp'), may hold values from 0.3 to 13.5
- offsets: int32 [4], replicated, may hold values from 0 to 3, each once
Outputs:
- query_grad: bfloat16 [4, 2, 4, 64, 4096], P('dp', 'seq', None, None, 'mp')
- key_grad: bfloat16 [4, 2, 4, 64, 4096], P('dp', 'seq', None, None, 'mp')
- value_grad: bfloat16 [4, 2, 4, 64, 4096], P('dp', 'seq', None, None, 'mp')
Inputs may be any that keep to these rules, and one draw needn't show every extreme that they name: `offsets`: every value from 0 to 3 occurs exactly once. `segments`: within a pack ids never fall and every id from 0 to 7 occurs; an image has at most 128 tokens and some image exactly that many.
All inputs are finite; a program needn't handle non-finite values.
Results may differ from a plain program's by a relative error of at most 0.012.
Values may be sent and summed in bfloat16 or wider, within the bound.
A program may use at most 64 MiB of HBM per device.

v0:
```python
import jax
import jax.numpy as jnp
from jax import lax
from jax.sharding import PartitionSpec as P

HD = 128


def for_sending(shard):

    def short(part):
        return part.astype(jnp.bfloat16) if part.dtype == jnp.float32 else part

    return jax.tree.map(short, shard)


def softmax_grads(q_rows, k_rows, v_rows, d_rows, image_ids):
    total_rows = q_rows.shape[0]
    block_rows = min(512, total_rows)
    factor = q_rows.shape[1] ** (-0.5)
    key_total = jnp.zeros(k_rows.shape, jnp.float32)
    value_total = jnp.zeros(v_rows.shape, jnp.float32)
    query_pieces = []
    for start_row in range(0, total_rows, block_rows):
        q_block = q_rows[start_row : start_row + block_rows]
        d_block = d_rows[start_row : start_row + block_rows]
        same_image = image_ids[start_row : start_row + block_rows, None] == image_ids[None, :]
        scores = (
            jnp.einsum("td,ud->tu", q_block, k_rows, preferred_element_type=jnp.float32) * factor
        )
        masked = jnp.where(same_image, scores, -1e30)
        row_top = jnp.max(masked, axis=1, keepdims=True)
        exponent = jnp.exp(masked - row_top)
        attention = exponent / jnp.sum(exponent, axis=1, keepdims=True)
        grad_attention = jnp.einsum(
            "td,ud->tu", d_block, v_rows, preferred_element_type=jnp.float32
        )
        row_inner = jnp.sum(attention * grad_attention, axis=1, keepdims=True)
        grad_scores = (attention * (grad_attention - row_inner) * factor).astype(jnp.bfloat16)
        query_pieces.append(
            jnp.einsum("tu,ud->td", grad_scores, k_rows, preferred_element_type=jnp.float32).astype(
                jnp.bfloat16
            )
        )
        key_total = key_total + jnp.einsum(
            "tu,td->ud", grad_scores, q_block, preferred_element_type=jnp.float32
        )
        value_total = value_total + jnp.einsum(
            "tu,td->ud", attention.astype(jnp.bfloat16), d_block, preferred_element_type=jnp.float32
        )
    return (
        jnp.concatenate(query_pieces, axis=0),
        key_total.astype(jnp.bfloat16),
        value_total.astype(jnp.bfloat16),
    )


def shards(queries, key_vectors, value_rows, upstream, segments, losses, offsets):
    pieces = queries.shape[2]
    piece_rows = queries.shape[3]
    columns = queries.shape[4]
    local_rows = pieces * piece_rows
    dp_count = lax.axis_size("dp")
    seq_count = lax.axis_size("seq")
    position = lax.axis_index("dp")
    dp_slots = jnp.arange(dp_count, dtype=jnp.int32)
    loss_sum = lax.psum(jnp.sum(losses), "dp")
    loss_mean = loss_sum / (losses.shape[1] * dp_count)
    image_weight = 2.0 / (1.0 + jnp.exp(losses[0] - loss_mean))
    image_ids = segments[0]
    image_slots = jnp.arange(losses.shape[1], dtype=jnp.int32)
    token_weight = jnp.sum(
        jnp.where(image_ids[:, None] == image_slots[None, :], image_weight[None, :], 0.0), axis=1
    )
    local_parts = tuple(
        (
            array.reshape(pieces, piece_rows, columns)
            for array in (queries, key_vectors, value_rows, upstream)
        )
    )
    targets = (position + offsets) % dp_count
    select = (targets[None, :] == dp_slots[:, None]).astype(jnp.bfloat16)
    outgoing = tuple(
        (
            jnp.einsum("nj,jrc->nrc", select, block, preferred_element_type=jnp.float32).astype(
                jnp.bfloat16
            )
            for block in local_parts
        )
    )
    incoming = (
        lax.all_to_all(outgoing[0], "dp", split_axis=0, concat_axis=0, tiled=True),
        lax.all_to_all(outgoing[1], "dp", split_axis=0, concat_axis=0, tiled=True),
        lax.all_to_all(outgoing[2], "dp", split_axis=0, concat_axis=0, tiled=True),
        lax.all_to_all(outgoing[3], "dp", split_axis=0, concat_axis=0, tiled=True),
    )
    sources = (position - offsets) % dp_count
    arrived = tuple((block[sources] for block in incoming))
    heads_each = columns // (seq_count * HD)
    grouped = tuple((block.reshape(local_rows, seq_count, heads_each, HD) for block in arrived))
    q_all = lax.all_to_all(grouped[0], "seq", split_axis=1, concat_axis=0, tiled=True)[:, 0]
    k_all = lax.all_to_all(grouped[1], "seq", split_axis=1, concat_axis=0, tiled=True)[:, 0]
    v_all = lax.all_to_all(grouped[2], "seq", split_axis=1, concat_axis=0, tiled=True)[:, 0]
    grad_out = (
        token_weight[:, None, None]
        * lax.all_to_all(grouped[3], "seq", split_axis=1, concat_axis=0, tiled=True)[:, 0].astype(
            jnp.float32
        )
    ).astype(jnp.bfloat16)
    grads = jax.vmap(softmax_grads, in_axes=(1, 1, 1, 1, None), out_axes=1)(
        q_all, k_all, v_all, grad_out, image_ids
    )
    results = tuple((item[:, None] for item in grads))
    returned = (
        lax.all_to_all(for_sending(results[0]), "seq", split_axis=0, concat_axis=1, tiled=True),
        lax.all_to_all(for_sending(results[1]), "seq", split_axis=0, concat_axis=1, tiled=True),
        lax.all_to_all(for_sending(results[2]), "seq", split_axis=0, concat_axis=1, tiled=True),
    )
    back_parts = tuple((block.reshape(pieces, piece_rows, columns) for block in returned))
    anchors = (position - offsets) % dp_count
    select_back = (anchors[None, :] == dp_slots[:, None]).astype(jnp.bfloat16)
    outgoing_back = tuple(
        (
            jnp.einsum(
                "nj,jrc->nrc", select_back, block, preferred_element_type=jnp.float32
            ).astype(jnp.bfloat16)
            for block in back_parts
        )
    )
    incoming_back = (
        lax.all_to_all(outgoing_back[0], "dp", split_axis=0, concat_axis=0, tiled=True),
        lax.all_to_all(outgoing_back[1], "dp", split_axis=0, concat_axis=0, tiled=True),
        lax.all_to_all(outgoing_back[2], "dp", split_axis=0, concat_axis=0, tiled=True),
    )
    destinations = (position + offsets) % dp_count
    finished = tuple((block[destinations] for block in incoming_back))
    return tuple((block.reshape(1, 1, pieces, piece_rows, columns) for block in finished))


def solution(mesh):
    placed = (
        P("dp", "seq", None, None, "mp"),
        P("dp", "seq", None, None, "mp"),
        P("dp", "seq", None, None, "mp"),
        P("dp", "seq", None, None, "mp"),
        P("dp", None),
        P("dp", None),
        P(),
    )
    return jax.shard_map(
        shards,
        mesh=mesh,
        in_specs=placed,
        out_specs=(
            P("dp", "seq", None, None, "mp"),
            P("dp", "seq", None, None, "mp"),
            P("dp", "seq", None, None, "mp"),
        ),
        check_vma=False,
    )
```

profile of v0, /device:TPU:0, one launch (start us, length us, event | category | flops | bytes accessed | tf_op | source)
XLA Modules:
  0.0 227.1 jit_solution(9145847461622189274)
XLA Ops:
  3.2 6.3 %all-to-all-start = ((bf16[4,64,1024]{2,1,0:T(8,128)(2,1)}), bf16[4,64,1024]{2,1,0:T(8,128)(2,1)S(1)}, u32[]{:S(2)}, u32[]{:S(2)}) async-start(bf16[4,64,1024]{2,1,0:T(8,128)(2,1)} %copy.91), calls=%async_computation | async-start | bytes 1048576 | tf_op jit(solution)/shard_map/all_to_all | solution.py:92
  12.0 12.0 %all-to-all-done = bf16[4,64,1024]{2,1,0:T(8,128)(2,1)S(1)} async-done(((bf16[4,64,1024]{2,1,0:T(8,128)(2,1)}), bf16[4,64,1024]{2,1,0:T(8,128)(2,1)S(1)}, u32[]{:S(2)}, u32[]{:S(2)}) %all-to-all-start) | async-done | bytes 524320 | tf_op jit(solution)/shard_map/all_to_all | solution.py:92
  28.9 12.5 %all-to-all-done.2 = bf16[4,64,1024]{2,1,0:T(8,128)(2,1)S(1)} async-done(((bf16[4,64,1024]{2,1,0:T(8,128)(2,1)}), bf16[4,64,1024]{2,1,0:T(8,128)(2,1)S(1)}, u32[]{:S(2)}, u32[]{:S(2)}) %all-to-all-start.2) | async-done | bytes 524320 | tf_op jit(solution)/shard_map/all_to_all | solution.py:93
  46.4 12.5 %all-to-all-done.4 = bf16[4,64,1024]{2,1,0:T(8,128)(2,1)S(1)} async-done(((bf16[4,64,1024]{2,1,0:T(8,128)(2,1)}), bf16[4,64,1024]{2,1,0:T(8,128)(2,1)S(1)}, u32[]{:S(2)}, u32[]{:S(2)}) %all-to-all-start.4) | async-done | bytes 524320 | tf_op jit(solution)/shard_map/all_to_all | solution.py:95
  64.3 12.0 %all-to-all-done.6 = bf16[4,64,1024]{2,1,0:T(8,128)(2,1)S(1)} async-done(((bf16[4,64,1024]{2,1,0:T(8,128)(2,1)}), bf16[4,64,1024]{2,1,0:T(8,128)(2,1)S(1)}, u32[]{:S(2)}, u32[]{:S(2)}) %all-to-all-start.6) | async-done | bytes 524320 | tf_op jit(solution)/shard_map/all_to_all | solution.py:94
  76.3 3.5 %all-to-all-start.1 = ((bf16[256,2,4,128]{3,2,0,1:T(4,128)(2,1)}), bf16[256,2,4,128]{3,2,0,1:T(4,128)(2,1)S(1)}, u32[]{:S(2)}, u32[]{:S(2)}) async-start(bf16[256,2,4,128]{3,2,0,1:T(4,128)(2,1)} %copy.92), calls=%async_computation.1 | async-start | bytes 1048576 | tf_op jit(solution)/shard_map/all_to_all | solution.py:101
  81.7 5.5 %all-to-all-done.1 = bf16[256,2,4,128]{3,2,0,1:T(4,128)(2,1)S(1)} async-done(((bf16[256,2,4,128]{3,2,0,1:T(4,128)(2,1)}), bf16[256,2,4,128]{3,2,0,1:T(4,128)(2,1)S(1)}, u32[]{:S(2)}, u32[]{:S(2)}) %all-to-all-start.1) | async-done | bytes 524320 | tf_op jit(solution)/shard_map/all_to_all | solution.py:101
  87.2 3.5 %all-to-all-start.3 = ((bf16[256,2,4,128]{3,2,0,1:T(4,128)(2,1)}), bf16[256,2,4,128]{3,2,0,1:T(4,128)(2,1)S(1)}, u32[]{:S(2)}, u32[]{:S(2)}) async-start(bf16[256,2,4,128]{3,2,0,1:T(4,128)(2,1)} %copy.96), calls=%async_computation.3 | async-start | bytes 1048576 | tf_op jit(solution)/shard_map/all_to_all | solution.py:102
  92.6 4.6 %all-to-all-done.3 = bf16[256,2,4,128]{3,2,0,1:T(4,128)(2,1)S(1)} async-done(((bf16[256,2,4,128]{3,2,0,1:T(4,128)(2,1)}), bf16[256,2,4,128]{3,2,0,1:T(4,128)(2,1)S(1)}, u32[]{:S(2)}, u32[]{:S(2)}) %all-to-all-start.3) | async-done | bytes 524320 | tf_op jit(solution)/shard_map/all_to_all | solution.py:102
  97.3 3.5 %all-to-all-start.7 = ((bf16[256,2,4,128]{3,2,0,1:T(4,128)(2,1)}), bf16[256,2,4,128]{3,2,0,1:T(4,128)(2,1)S(1)}, u32[]{:S(2)}, u32[]{:S(2)}) async-start(bf16[256,2,4,128]{3,2,0,1:T(4,128)(2,1)} %copy.104), calls=%async_computation.7 | async-start | bytes 1048576 | tf_op jit(solution)/shard_map/all_to_all | solution.py:103
  101.4 9.8 %psum.7 = f32[]{:T(128)} all-reduce(f32[]{:T(128)} %reduce_sum.37), channel_id=1, replica_groups=mesh['dp'=4,'seq'=2,'mp'=4] {'dp'}, use_global_device_ids=true, to_apply=%region_3.4 | all-reduce | flops 1 | bytes 8 | tf_op jit(solution)/shard_map/psum | solution.py:67
  113.7 3.5 %all-to-all-start.5 = ((bf16[256,2,4,128]{3,2,0,1:T(4,128)(2,1)}), bf16[256,2,4,128]{3,2,0,1:T(4,128)(2,1)S(1)}, u32[]{:S(2)}, u32[]{:S(2)}) async-start(bf16[256,2,4,128]{3,2,0,1:T(4,128)(2,1)} %copy.100), calls=%async_computation.5 | async-start | bytes 1048576 | tf_op jit(solution)/shard_map/all_to_all | solution.py:106
  119.4 4.4 %all-to-all-done.5 = bf16[256,2,4,128]{3,2,0,1:T(4,128)(2,1)S(1)} async-done(((bf16[256,2,4,128]{3,2,0,1:T(4,128)(2,1)}), bf16[256,2,4,128]{3,2,0,1:T(4,128)(2,1)S(1)}, u32[]{:S(2)}, u32[]{:S(2)}) %all-to-all-start.5) | async-done | bytes 524320 | tf_op jit(solution)/shard_map/all_to_all | solution.py:106
  126.7 4.7 %fusion.64 = (f32[4,512]{1,0:T(4,128)S(1)}, f32[4,512,512]{1,2,0:T(8,128)}) fusion(pred[512,512]{0,1:T(8,128)(4,1)S(1)} %broadcast_compare_fusion, bf16[512,4,128]{2,0,1:T(8,128)(2,1)} %bitcast.91, bf16[512,4,128]{2,0,1:T(8,128)(2,1)S(1)} %bitcast.89), kind=kOutput, calls=%fused_computation.78 | convolution fusion | flops 272630272 | bytes 5513216 | tf_op jit(solution)/shard_map/vmap()/sub | solution.py:33
  131.4 7.6 %fusion.28 = bf16[512,1,4,128]{3,0,2,1:T(8,128)(2,1)S(1)} fusion(bf16[512,4,128]{2,0,1:T(8,128)(2,1)S(1)} %bitcast.92, f32[4,512,512]{1,2,0:T(8,128)} %fusion.63, f32[4,512,512]{1,2,0:T(8,128)} %get-tuple-element.13, f32[4,512]{1,0:T(4,128)S(1)} %get-tuple-element.12), kind=kOutput, calls=%fused_computation.35 | convolution fusion | flops 276040192 | bytes 9445376 | tf_op jit(solution)/shard_map/vmap(tu,td->ud)/dot_general | solution.py:45
  140.3 3.7 %all-to-all-start.10 = ((bf16[512,1,4,128]{3,2,1,0:T(4,128)(2,1)}), bf16[512,1,4,128]{3,2,1,0:T(4,128)(2,1)S(1)}, u32[]{:S(2)}, u32[]{:S(2)}) async-start(bf16[512,1,4,128]{3,2,1,0:T(4,128)(2,1)} %copy.111), calls=%async_computation.10 | async-start | bytes 1048576 | tf_op jit(solution)/shard_map/all_to_all | solution.py:116
  143.9 8.0 %fusion.31 = bf16[512,1,4,128]{3,0,2,1:T(8,128)(2,1)S(1)} fusion(bf16[512,4,128]{2,0,1:T(8,128)(2,1)S(1)} %bitcast.90, f32[4,512,512]{1,2,0:T(8,128)} %fusion.63, f32[4,512,512]{1,2,0:T(8,128)} %get-tuple-element.13, f32[4,512]{1,0:T(4,128)S(1)} %get-tuple-element.12), kind=kOutput, calls=%fused_computation.36 | convolution fusion | flops 276040192 | bytes 9445376 | tf_op jit(solution)/shard_map/vmap(tu,ud->td)/dot_general | solution.py:41
  153.1 3.5 %all-to-all-start.8 = ((bf16[512,1,4,128]{3,2,1,0:T(4,128)(2,1)}), bf16[512,1,4,128]{3,2,1,0:T(4,128)(2,1)S(1)}, u32[]{:S(2)}, u32[]{:S(2)}) async-start(bf16[512,1,4,128]{3,2,1,0:T(4,128)(2,1)} %copy.107), calls=%async_computation.8 | async-start | bytes 1048576 | tf_op jit(solution)/shard_map/all_to_all | solution.py:115
  160.8 3.9 %all-to-all-done.8 = bf16[512,1,4,128]{3,2,1,0:T(4,128)(2,1)S(1)} async-done(((bf16[512,1,4,128]{3,2,1,0:T(4,128)(2,1)}), bf16[512,1,4,128]{3,2,1,0:T(4,128)(2,1)S(1)}, u32[]{:S(2)}, u32[]{:S(2)}) %all-to-all-start.8) | async-done | bytes 524320 | tf_op jit(solution)/shard_map/all_to_all | solution.py:115
  164.7 3.5 %all-to-all-start.12 = ((bf16[512,1,4,128]{3,2,1,0:T(4,128)(2,1)}), bf16[512,1,4,128]{3,2,1,0:T(4,128)(2,1)S(1)}, u32[]{:S(2)}, u32[]{:S(2)}) async-start(bf16[512,1,4,128]{3,2,1,0:T(4,128)(2,1)} %copy.115), calls=%async_computation.12 | async-start | bytes 1048576 | tf_op jit(solution)/shard_map/all_to_all | solution.py:117
  170.2 4.5 %all-to-all-done.12 = bf16[512,1,4,128]{3,2,1,0:T(4,128)(2,1)S(1)} async-done(((bf16[512,1,4,128]{3,2,1,0:T(4,128)(2,1)}), bf16[512,1,4,128]{3,2,1,0:T(4,128)(2,1)S(1)}, u32[]{:S(2)}, u32[]{:S(2)}) %all-to-all-start.12) | async-done | bytes 524320 | tf_op jit(solution)/shard_map/all_to_all | solution.py:117
  180.3 12.5 %all-to-all-done.11 = bf16[4,64,1024]{2,1,0:T(8,128)(2,1)S(1)} async-done(((bf16[4,64,1024]{2,1,0:T(8,128)(2,1)}), bf16[4,64,1024]{2,1,0:T(8,128)(2,1)S(1)}, u32[]{:S(2)}, u32[]{:S(2)}) %all-to-all-start.11) | async-done | bytes 524320 | tf_op jit(solution)/shard_map/all_to_all | solution.py:132
  198.3 13.7 %all-to-all-done.9 = bf16[4,64,1024]{2,1,0:T(8,128)(2,1)S(1)} async-done(((bf16[4,64,1024]{2,1,0:T(8,128)(2,1)}), bf16[4,64,1024]{2,1,0:T(8,128)(2,1)S(1)}, u32[]{:S(2)}, u32[]{:S(2)}) %all-to-all-start.9) | async-done | bytes 524320 | tf_op jit(solution)/shard_map/all_to_all | solution.py:131
  218.2 7.5 %all-to-all-done.13 = bf16[4,64,1024]{2,1,0:T(8,128)(2,1)S(1)} async-done(((bf16[4,64,1024]{2,1,0:T(8,128)(2,1)}), bf16[4,64,1024]{2,1,0:T(8,128)(2,1)S(1)}, u32[]{:S(2)}, u32[]{:S(2)}) %all-to-all-start.13) | async-done | bytes 524320 | tf_op jit(solution)/shard_map/all_to_all | solution.py:133
  (73 shorter events, 58.7 us)
Async XLA Ops:
  0.6 1.1 copy-start
  0.6 26.8 %copy-start.4 = (bf16[1,1,4,64,1024]{4,3,2,1,0:T(8,128)(2,1)S(1)}, bf16[1,1,4,64,1024]{4,3,2,1,0:T(8,128)(2,1)}, u32[]{:S(2)}) copy-start(bf16[1,1,4,64,1024]{4,3,2,1,0:T(8,128)(2,1)} %param.10) | copy-start | bytes 1572868
  2.2 42.7 %copy-start.5 = (bf16[1,1,4,64,1024]{4,3,2,1,0:T(8,128)(2,1)S(1)}, bf16[1,1,4,64,1024]{4,3,2,1,0:T(8,128)(2,1)}, u32[]{:S(2)}) copy-start(bf16[1,1,4,64,1024]{4,3,2,1,0:T(8,128)(2,1)} %param.9) | copy-start | bytes 1572868
  3.2 20.8 %all-to-all-start = ((bf16[4,64,1024]{2,1,0:T(8,128)(2,1)}), bf16[4,64,1024]{2,1,0:T(8,128)(2,1)S(1)}, u32[]{:S(2)}, u32[]{:S(2)}) async-start(bf16[4,64,1024]{2,1,0:T(8,128)(2,1)} %copy.91), calls=%async_computation | async-start | bytes 1048576 | tf_op jit(solution)/shard_map/all_to_all | solution.py:92
  24.0 17.4 %all-to-all-start.2 = ((bf16[4,64,1024]{2,1,0:T(8,128)(2,1)}), bf16[4,64,1024]{2,1,0:T(8,128)(2,1)S(1)}, u32[]{:S(2)}, u32[]{:S(2)}) async-start(bf16[4,64,1024]{2,1,0:T(8,128)(2,1)} %copy.95), calls=%async_computation.2 | async-start | bytes 1048576 | tf_op jit(solution)/shard_map/all_to_all | solution.py:93
  41.4 17.4 %all-to-all-start.4 = ((bf16[4,64,1024]{2,1,0:T(8,128)(2,1)}), bf16[4,64,1024]{2,1,0:T(8,128)(2,1)S(1)}, u32[]{:S(2)}, u32[]{:S(2)}) async-start(bf16[4,64,1024]{2,1,0:T(8,128)(2,1)} %copy.99), calls=%async_computation.4 | async-start | bytes 1048576 | tf_op jit(solution)/shard_map/all_to_all | solution.py:95
  58.8 17.4 %all-to-all-start.6 = ((bf16[4,64,1024]{2,1,0:T(8,128)(2,1)}), bf16[4,64,1024]{2,1,0:T(8,128)(2,1)S(1)}, u32[]{:S(2)}, u32[]{:S(2)}) async-start(bf16[4,64,1024]{2,1,0:T(8,128)(2,1)} %copy.103), calls=%async_computation.6 | async-start | bytes 1048576 | tf_op jit(solution)/shard_map/all_to_all | solution.py:94
  76.3 10.9 %all-to-all-start.1 = ((bf16[256,2,4,128]{3,2,0,1:T(4,128)(2,1)}), bf16[256,2,4,128]{3,2,0,1:T(4,128)(2,1)S(1)}, u32[]{:S(2)}, u32[]{:S(2)}) async-start(bf16[256,2,4,128]{3,2,0,1:T(4,128)(2,1)} %copy.92), calls=%async_computation.1 | async-start | bytes 1048576 | tf_op jit(solution)/shard_map/all_to_all | solution.py:101
  79.8 21.0 %copy-start.6 = (f32[1,8]{1,0:T(1,128)S(1)}, f32[1,8]{1,0:T(1,128)}, u32[]{:S(2)}) copy-start(f32[1,8]{1,0:T(1,128)} %param.12) | copy-start | bytes 100
  87.2 10.1 %all-to-all-start.3 = ((bf16[256,2,4,128]{3,2,0,1:T(4,128)(2,1)}), bf16[256,2,4,128]{3,2,0,1:T(4,128)(2,1)S(1)}, u32[]{:S(2)}, u32[]{:S(2)}) async-start(bf16[256,2,4,128]{3,2,0,1:T(4,128)(2,1)} %copy.96), calls=%async_computation.3 | async-start | bytes 1048576 | tf_op jit(solution)/shard_map/all_to_all | solution.py:102
  90.7 26.5 %copy-start.3 = (s32[1,512]{1,0:T(1,128)S(1)}, s32[1,512]{1,0:T(1,128)}, u32[]{:S(2)}) copy-start(s32[1,512]{1,0:T(1,128)} %param.11) | copy-start | bytes 6148
  97.3 16.5 %all-to-all-start.7 = ((bf16[256,2,4,128]{3,2,0,1:T(4,128)(2,1)}), bf16[256,2,4,128]{3,2,0,1:T(4,128)(2,1)S(1)}, u32[]{:S(2)}, u32[]{:S(2)}) async-start(bf16[256,2,4,128]{3,2,0,1:T(4,128)(2,1)} %copy.104), calls=%async_computation.7 | async-start | bytes 1048576 | tf_op jit(solution)/shard_map/all_to_all | solution.py:103
  113.7 10.1 %all-to-all-start.5 = ((bf16[256,2,4,128]{3,2,0,1:T(4,128)(2,1)}), bf16[256,2,4,128]{3,2,0,1:T(4,128)(2,1)S(1)}, u32[]{:S(2)}, u32[]{:S(2)}) async-start(bf16[256,2,4,128]{3,2,0,1:T(4,128)(2,1)} %copy.100), calls=%async_computation.5 | async-start | bytes 1048576 | tf_op jit(solution)/shard_map/all_to_all | solution.py:106
  119.4 7.3 %copy-start.1 = (bf16[2,256,1,4,128]{4,1,0,3,2:T(8,128)(2,1)S(1)}, bf16[2,256,1,4,128]{4,1,0,3,2:T(8,128)(2,1)}, u32[]{:S(2)}) copy-start(bf16[2,256,1,4,128]{4,1,0,3,2:T(8,128)(2,1)} %copy.97) | copy-start | bytes 1572868
  126.7 4.8 %copy-start.2 = (bf16[2,256,1,4,128]{4,1,0,3,2:T(8,128)(2,1)S(1)}, bf16[2,256,1,4,128]{4,1,0,3,2:T(8,128)(2,1)}, u32[]{:S(2)}) copy-start(bf16[2,256,1,4,128]{4,1,0,3,2:T(8,128)(2,1)} %copy.93) | copy-start | bytes 1572868
  140.3 12.9 %all-to-all-start.10 = ((bf16[512,1,4,128]{3,2,1,0:T(4,128)(2,1)}), bf16[512,1,4,128]{3,2,1,0:T(4,128)(2,1)S(1)}, u32[]{:S(2)}, u32[]{:S(2)}) async-start(bf16[512,1,4,128]{3,2,1,0:T(4,128)(2,1)} %copy.111), calls=%async_computation.10 | async-start | bytes 1048576 | tf_op jit(solution)/shard_map/all_to_all | solution.py:116
  153.1 11.6 %all-to-all-start.8 = ((bf16[512,1,4,128]{3,2,1,0:T(4,128)(2,1)}), bf16[512,1,4,128]{3,2,1,0:T(4,128)(2,1)S(1)}, u32[]{:S(2)}, u32[]{:S(2)}) async-start(bf16[512,1,4,128]{3,2,1,0:T(4,128)(2,1)} %copy.107), calls=%async_computation.8 | async-start | bytes 1048576 | tf_op jit(solution)/shard_map/all_to_all | solution.py:115
  164.7 10.1 %all-to-all-start.12 = ((bf16[512,1,4,128]{3,2,1,0:T(4,128)(2,1)}), bf16[512,1,4,128]{3,2,1,0:T(4,128)(2,1)S(1)}, u32[]{:S(2)}, u32[]{:S(2)}) async-start(bf16[512,1,4,128]{3,2,1,0:T(4,128)(2,1)} %copy.115), calls=%async_computation.12 | async-start | bytes 1048576 | tf_op jit(solution)/shard_map/all_to_all | solution.py:117
  174.8 18.0 %all-to-all-start.11 = ((bf16[4,64,1024]{2,1,0:T(8,128)(2,1)}), bf16[4,64,1024]{2,1,0:T(8,128)(2,1)S(1)}, u32[]{:S(2)}, u32[]{:S(2)}) async-start(bf16[4,64,1024]{2,1,0:T(8,128)(2,1)} %copy.114), calls=%async_computation.11 | async-start | bytes 1048576 | tf_op jit(solution)/shard_map/all_to_all | solution.py:132
  192.8 19.2 %all-to-all-start.9 = ((bf16[4,64,1024]{2,1,0:T(8,128)(2,1)}), bf16[4,64,1024]{2,1,0:T(8,128)(2,1)S(1)}, u32[]{:S(2)}, u32[]{:S(2)}) async-start(bf16[4,64,1024]{2,1,0:T(8,128)(2,1)} %copy.110), calls=%async_computation.9 | async-start | bytes 1048576 | tf_op jit(solution)/shard_map/all_to_all | solution.py:131
  212.0 13.7 %all-to-all-start.13 = ((bf16[4,64,1024]{2,1,0:T(8,128)(2,1)}), bf16[4,64,1024]{2,1,0:T(8,128)(2,1)S(1)}, u32[]{:S(2)}, u32[]{:S(2)}) async-start(bf16[4,64,1024]{2,1,0:T(8,128)(2,1)} %copy.118), calls=%async_computation.13 | async-start | bytes 1048576 | tf_op jit(solution)/shard_map/all_to_all | solution.py:133
where the time goes:
time: 228 us; the launch traced here: 227 us
  waiting for transfers between devices  106 us (46%)
  starting transfers between devices  51.8 us (23%)
  matrix products  30.6 us (13%)
  local copies, waits for them, and re-layouts  25.9 us (11%)
  blocking collectives  9.75 us (4%)
    all_to_all x1, waiting for transfers between devices, shards(): lax.all_to_all(outgoing_back[0], 'dp', split_axis=0, concat_axis=0, tiled...  13.7 us
    all_to_all x1, waiting for transfers between devices, shards(): lax.all_to_all(outgoing_back[1], 'dp', split_axis=0, concat_axis=0, tiled...  12.5 us
    all_to_all x1, waiting for transfers between devices, shards(): lax.all_to_all(outgoing[1], 'dp', split_axis=0, concat_axis=0, tiled=True)  12.5 us
    all_to_all x1, waiting for transfers between devices, shards(): lax.all_to_all(outgoing[3], 'dp', split_axis=0, concat_axis=0, tiled=True)  12.5 us
    all_to_all x1, waiting for transfers between devices, shards(): lax.all_to_all(outgoing[0], 'dp', split_axis=0, concat_axis=0, tiled=True)  12 us
    all_to_all x1, waiting for transfers between devices, shards(): lax.all_to_all(outgoing[2], 'dp', split_axis=0, concat_axis=0, tiled=True)  12 us
    psum x1, blocking collectives, shards(): loss_sum = lax.psum(jnp.sum(losses), 'dp')  9.75 us
    dot_general x1, matrix products, softmax_grads(): jnp.einsum('tu,ud->td', grad_scores, k_rows, preferred_element_type=jnp.f...  7.97 us
  transfers between devices with their start and end apart: 14, of which 12 were waited for; matrix products, arithmetic and copies ran while one was open for 17% of the time, Pallas kernels for 0%

commit v1 on v0

--- a/solution.py
+++ b/solution.py
@@ -1,6 +1,11 @@
+import functools
+import math
+
 import jax
 import jax.numpy as jnp
 from jax import lax
+from jax.experimental import pallas as pl
+from jax.experimental.pallas import tpu as pltpu
 from jax.sharding import PartitionSpec as P
 
 HD = 128
@@ -12,6 +17,13 @@
         return part.astype(jnp.bfloat16) if part.dtype == jnp.float32 else part
 
     return jax.tree.map(short, shard)
+
+
+def picked(block, slots):
+    chosen = (slots[:, None] == jnp.arange(block.shape[0])[None, :]).astype(jnp.bfloat16)
+    return jnp.einsum("jn,nrc->jrc", chosen, block, preferred_element_type=jnp.float32).astype(
+        jnp.bfloat16
+    )
 
 
 def softmax_grads(q_rows, k_rows, v_rows, d_rows, image_ids):
@@ -55,7 +67,7 @@
     )
 
 
-def shards(queries, key_vectors, value_rows, upstream, segments, losses, offsets):
+def plain_shards(queries, key_vectors, value_rows, upstream, segments, losses, offsets):
     pieces = queries.shape[2]
     piece_rows = queries.shape[3]
     columns = queries.shape[4]
@@ -95,7 +107,7 @@
         lax.all_to_all(outgoing[3], "dp", split_axis=0, concat_axis=0, tiled=True),
     )
     sources = (position - offsets) % dp_count
-    arrived = tuple((block[sources] for block in incoming))
+    arrived = tuple((picked(block, sources) for block in incoming))
     heads_each = columns // (seq_count * HD)
     grouped = tuple((block.reshape(local_rows, seq_count, heads_each, HD) for block in arrived))
     q_all = lax.all_to_all(grouped[0], "seq", split_axis=1, concat_axis=0, tiled=True)[:, 0]
@@ -133,8 +145,278 @@
         lax.all_to_all(outgoing_back[2], "dp", split_axis=0, concat_axis=0, tiled=True),
     )
     destinations = (position + offsets) % dp_count
-    finished = tuple((block[destinations] for block in incoming_back))
+    finished = tuple((picked(block, destinations) for block in incoming_back))
     return tuple((block.reshape(1, 1, pieces, piece_rows, columns) for block in finished))
+
+
+MESH = pl.DeviceIdType.MESH
+
+
+def dot_nt(a, b):
+    return lax.dot_general(a, b, (((1,), (1,)), ((), ())), preferred_element_type=jnp.float32)
+
+
+def dot_tn(a, b):
+    return lax.dot_general(a, b, (((0,), (0,)), ((), ())), preferred_element_type=jnp.float32)
+
+
+def exchange_kernel(
+    n_dp,
+    n_seq,
+    pieces,
+    rows,
+    heads_each,
+    images,
+    offsets_ref,
+    segments_ref,
+    losses_ref,
+    q_ref,
+    k_ref,
+    v_ref,
+    d_ref,
+    dq_ref,
+    dk_ref,
+    dv_ref,
+    *scratch,
+):
+    (send, recv, back_send, loss_send, loss_recv, ids_row, weight) = scratch[:7]
+    back_recv = scratch[7 : 7 + heads_each]
+    send_sem, recv_sem, back_send_sem, back_recv_sem, loss_send_sem, loss_recv_sem = scratch[
+        7 + heads_each :
+    ]
+    z = lax.axis_index("dp")
+    x = lax.axis_index("seq")
+    me = z * n_seq + x
+    parts = n_dp * n_seq
+    total = parts * rows
+    factor = HD**-0.5
+    log2e = math.log2(math.e)
+
+    dp_shifts = sorted(range(n_dp), key=lambda s: -min(s, n_dp - s))
+    all_shifts = [(a, b) for a in dp_shifts for b in reversed(range(n_seq))]
+    partners = []
+    for a, b in all_shifts[:-1]:
+        pz, px = lax.rem(z + a, n_dp), lax.rem(x + b, n_seq)
+        partners.append((pz, px, pz * n_seq + px))
+
+    barrier = pltpu.get_barrier_semaphore()
+    for pz, px, _ in partners:
+        pl.semaphore_signal(
+            barrier, inc=1, device_id={"dp": pz, "seq": px}, device_id_type=MESH
+        )
+
+    offset = [offsets_ref[j] for j in range(pieces)]
+
+    def group_with(shift):
+        found = jnp.int32(0)
+        for j in range(1, pieces):
+            found = jnp.where(offset[j] == shift, jnp.int32(j), found)
+        return found
+
+    taken = [group_with(lax.rem(n - z + n_dp, n_dp)) for n in range(n_dp)]
+
+    def stage(c):
+        for n in range(n_dp):
+            for s in range(n_seq):
+                cols = slice((s * heads_each + c) * HD, (s * heads_each + c + 1) * HD)
+                for i, ref in enumerate((q_ref, k_ref, v_ref, d_ref)):
+                    send[c, n * n_seq + s, i] = ref[taken[n], :, cols]
+
+    def send_copy(c, pz, px, m):
+        return pltpu.make_async_remote_copy(
+            src_ref=send.at[c, m],
+            dst_ref=recv.at[c, me],
+            send_sem=send_sem.at[c, m],
+            recv_sem=recv_sem.at[c, me],
+            device_id={"dp": pz, "seq": px},
+            device_id_type=MESH,
+        )
+
+    def recv_copy(c, pz, px, m):
+        return pltpu.make_async_remote_copy(
+            src_ref=send.at[c, m],
+            dst_ref=recv.at[c, m],
+            send_sem=send_sem.at[c, m],
+            recv_sem=recv_sem.at[c, m],
+            device_id={"dp": pz, "seq": px},
+            device_id_type=MESH,
+        )
+
+    def back_copy(c, pz, px, m):
+        return pltpu.make_async_remote_copy(
+            src_ref=back_send.at[c, m],
+            dst_ref=back_recv[c].at[me],
+            send_sem=back_send_sem.at[c, m],
+            recv_sem=back_recv_sem.at[c, me],
+            device_id={"dp": pz, "seq": px},
+            device_id_type=MESH,
+        )
+
+    def back_arrival(c, pz, px, m):
+        return pltpu.make_async_remote_copy(
+            src_ref=back_send.at[c, m],
+            dst_ref=back_recv[c].at[m],
+            send_sem=back_send_sem.at[c, m],
+            recv_sem=back_recv_sem.at[c, m],
+            device_id={"dp": pz, "seq": px},
+            device_id_type=MESH,
+        )
+
+    def loss_copy(step, mine):
+        to = lax.rem(z + step, n_dp)
+        slot = z if mine else to
+        return pltpu.make_async_remote_copy(
+            src_ref=loss_send,
+            dst_ref=loss_recv.at[slot],
+            send_sem=loss_send_sem.at[step],
+            recv_sem=loss_recv_sem.at[slot],
+            device_id={"dp": to},
+            device_id_type=MESH,
+        )
+
+    loss_send[...] = jnp.zeros_like(loss_send)
+    loss_send[0:1, 0:images] = losses_ref[...]
+    loss_recv[z] = jnp.zeros(loss_send.shape, jnp.float32)
+    loss_recv[z, 0:1, 0:images] = losses_ref[...]
+
+    stage(0)
+    pl.semaphore_wait(barrier, parts - 1)
+    for step in range(1, n_dp):
+        loss_copy(step, True).start()
+    for c in range(heads_each):
+        if c:
+            stage(c)
+        for pz, px, m in partners:
+            send_copy(c, pz, px, m).start()
+
+    for d in range(n_dp):
+        shift = lax.rem(z - d + n_dp, n_dp)
+        for s in range(n_seq):
+            found = jnp.zeros((1, rows), jnp.int32)
+            for j in range(pieces):
+                at = (s * pieces + j) * rows
+                found = found + jnp.where(
+                    offset[j] == shift, segments_ref[0:1, at : at + rows], 0
+                )
+            m = d * n_seq + s
+            ids_row[0:1, m * rows : (m + 1) * rows] = found.astype(jnp.float32)
+    row_ids = ids_row[0:1, :]
+    column_ids = jnp.transpose(jnp.broadcast_to(row_ids, (8, total)))[:, 0:1]
+
+    for step in range(1, n_dp):
+        loss_copy(step, False).wait_recv()
+    loss_total = loss_recv[0]
+    for d in range(1, n_dp):
+        loss_total = loss_total + loss_recv[d]
+    loss_mean = jnp.sum(loss_total) / (images * n_dp)
+    image_weight = 2.0 / (1.0 + jnp.exp(losses_ref[...] - loss_mean))
+    slots = lax.broadcasted_iota(jnp.int32, (total, images), 1).astype(jnp.float32)
+    token_weight = jnp.sum(
+        jnp.where(column_ids == slots, image_weight, 0.0), axis=1, keepdims=True
+    )
+    weight[...] = jnp.broadcast_to(token_weight, (total, HD))
+
+    def work(c):
+        recv[c, me] = send[c, me]
+        for pz, px, m in partners:
+            recv_copy(c, pz, px, m).wait_recv()
+        q, k, v, d = (recv[c, :, i].reshape(total, HD) for i in range(4))
+        d = (weight[...] * d.astype(jnp.float32)).astype(jnp.bfloat16)
+        block = min(256, total)
+        k_sum = v_sum = None
+        per = block // rows
+        for b in range(total // block):
+            at = slice(b * block, (b + 1) * block)
+            same = column_ids[at] == row_ids
+            scores = jnp.where(same, dot_nt(q[at], k), -1e30)
+            top = jnp.max(scores, axis=1, keepdims=True)
+            e = jnp.exp2((scores - top) * (factor * log2e))
+            p = e * (1.0 / jnp.sum(e, axis=1, keepdims=True))
+            ga = dot_nt(d[at], v)
+            inner = jnp.sum(p * ga, axis=1, keepdims=True)
+            gs = (p * ((ga - inner) * factor)).astype(jnp.bfloat16)
+            dq = jnp.dot(gs, k, preferred_element_type=jnp.float32).astype(jnp.bfloat16)
+            back_send[c, b * per : (b + 1) * per, 0] = dq.reshape(per, rows, HD)
+            k_part = dot_tn(gs, q[at])
+            v_part = dot_tn(p.astype(jnp.bfloat16), d[at])
+            k_sum = k_part if b == 0 else k_sum + k_part
+            v_sum = v_part if b == 0 else v_sum + v_part
+        back_send[c, :, 1] = k_sum.astype(jnp.bfloat16).reshape(parts, rows, HD)
+        back_send[c, :, 2] = v_sum.astype(jnp.bfloat16).reshape(parts, rows, HD)
+
+    for c in range(heads_each):
+        work(c)
+        for pz, px, m in partners:
+            back_copy(c, pz, px, m).start()
+
+    packs = [lax.rem(z + offset[j], n_dp) for j in range(pieces)]
+    for c in range(heads_each):
+        back_recv[c][me] = back_send[c, me]
+        for pz, px, m in partners:
+            back_arrival(c, pz, px, m).wait_recv()
+        for s in range(n_seq):
+            cols = slice((s * heads_each + c) * HD, (s * heads_each + c + 1) * HD)
+            for j in range(pieces):
+                for i, ref in enumerate((dq_ref, dk_ref, dv_ref)):
+                    ref[j, :, cols] = back_recv[c][packs[j] * n_seq + s, i]
+
+    for step in range(1, n_dp):
+        loss_copy(step, True).wait_send()
+    for c in range(heads_each):
+        for pz, px, m in partners:
+            send_copy(c, pz, px, m).wait_send()
+            back_copy(c, pz, px, m).wait_send()
+
+
+def kernel_shards(queries, key_vectors, value_rows, upstream, segments, losses, offsets):
+    pieces, rows, columns = queries.shape[2:]
+    n_dp = lax.axis_size("dp")
+    n_seq = lax.axis_size("seq")
+    heads_each = columns // (n_seq * HD)
+    images = losses.shape[1]
+    parts = n_dp * n_seq
+    arrays = tuple(
+        a.reshape(pieces, rows, columns) for a in (queries, key_vectors, value_rows, upstream)
+    )
+    whole = pl.BlockSpec(memory_space=pltpu.VMEM)
+    result = jax.ShapeDtypeStruct((pieces, rows, columns), jnp.bfloat16)
+    dma = pltpu.SemaphoreType.DMA
+    grads = pl.pallas_call(
+        functools.partial(exchange_kernel, n_dp, n_seq, pieces, rows, heads_each, images),
+        out_shape=(result,) * 3,
+        in_specs=[pl.BlockSpec(memory_space=pltpu.SMEM)] + [whole] * 6,
+        out_specs=(whole,) * 3,
+        scratch_shapes=[
+            pltpu.VMEM((heads_each, parts, 4, rows, HD), jnp.bfloat16),
+            pltpu.VMEM((heads_each, parts, 4, rows, HD), jnp.bfloat16),
+            pltpu.VMEM((heads_each, parts, 3, rows, HD), jnp.bfloat16),
+            pltpu.VMEM((8, 128), jnp.float32),
+            pltpu.VMEM((n_dp, 8, 128), jnp.float32),
+            pltpu.VMEM((8, parts * rows), jnp.float32),
+            pltpu.VMEM((parts * rows, HD), jnp.float32),
+        ]
+        + [pltpu.VMEM((parts, 3, rows, HD), jnp.bfloat16)] * heads_each
+        + [
+            dma((heads_each, parts)),
+            dma((heads_each, parts)),
+            dma((heads_each, parts)),
+            dma((heads_each, parts)),
+            dma((n_dp,)),
+            dma((n_dp,)),
+        ],
+        compiler_params=pltpu.CompilerParams(
+            collective_id=0, has_side_effects=True, vmem_limit_bytes=48 * 1024 * 1024
+        ),
+    )(offsets, segments, losses, *arrays)
+    return tuple(g.reshape(1, 1, pieces, rows, columns) for g in grads)
+
+
+def shards(*arrays):
+    rows = arrays[0].shape[3]
+    partners = lax.axis_size("dp") * lax.axis_size("seq")
+    if rows % 16 == 0 and partners <= 8:
+        return kernel_shards(*arrays)
+    return plain_shards(*arrays)
 
 
 def solution(mesh):

time: 228 us -> 94.2 us (0.41)
  waiting for transfers between devices: 106 us -> 0 us
  Pallas kernels: 0 us -> 86 us
  starting transfers between devices: 51.8 us -> 0 us
  matrix products: 30.6 us -> 0 us
  local copies, waits for them, and re-layouts: 25.9 us -> 7.21 us
  blocking collectives: 9.75 us -> 0 us
    all_to_all x14 -> x0, waiting for transfers between devices: 106 us -> none  [the longest x1 13.7 us: shards(): lax.all_to_all(outgoing_back[0], 'dp', split_axis=0, concat_axis=0, tiled...]
    pallas_call x0 -> x1, Pallas kernels: none -> 86 us  [kernel_shards(): pl.pallas_call(functools.partial(exchange_kernel, n_dp, n_seq, pieces, ro...]
    all_to_all x14 -> x0, starting transfers between devices: 51.8 us -> none  [the longest x1 6.31 us: shards(): lax.all_to_all(outgoing[0], 'dp', split_axis=0, concat_axis=0, tiled=True)]
    dot_general x11 -> x0, matrix products: 25.9 us -> none  [the longest x1 7.97 us: softmax_grads(): jnp.einsum('tu,ud->td', grad_scores, k_rows, preferred_element_type=jnp.f...]
    psum x1 -> x0, blocking collectives: 9.75 us -> none  [shards(): loss_sum = lax.psum(jnp.sum(losses), 'dp')]
    unnamed x14 -> x17, local copies, waits for them, and re-layouts: 0.32 us -> 7.21 us
    convert_element_type x7 -> x0, local copies, waits for them, and re-layouts: 6.68 us -> none  [the longest x4 3.82 us: shards(): jnp.einsum('nj,jrc->nrc', select, block, preferred_element_type=jnp.float32)]
    reshape x11 -> x0, local copies, waits for them, and re-layouts: 6.46 us -> none  [the longest x8 5.36 us: shards(): block.reshape(local_rows, seq_count, heads_each, HD)]
  transfers between devices with their start and end apart: 14 -> 0, of which waited for: 12 -> 0; matrix products, arithmetic and copies ran while one was open for 17% -> 0% of each run, Pallas kernels for 0% -> 0%
where the time goes in v1:
time: 94.2 us; the launch traced here: 93.9 us
  Pallas kernels  86 us (91%)
  local copies, waits for them, and re-layouts  7.21 us (8%)
    pallas_call x1, Pallas kernels, kernel_shards(): pl.pallas_call(functools.partial(exchange_kernel, n_dp, n_seq, pieces, ro...  86 us
    unnamed x17, local copies, waits for them, and re-layouts  7.21 us

profile of v1, /device:TPU:0, one launch (start us, length us, event | category | flops | bytes accessed | tf_op | source)
XLA Modules:
  0.0 93.9 jit_solution(14434834700092093660)
XLA Ops:
  0.6 0.0 copy-start.4
  0.6 0.0 copy-start.5
  0.7 0.0 copy-start.6
  0.7 0.7 copy-done.4
  1.3 0.0 copy-done.5
  1.3 0.0 copy-done.6
  1.3 0.0 copy-start
  1.3 1.0 %copy-done = bf16[1,1,4,64,1024]{4,3,2,1,0:T(8,128)(2,1)S(1)} copy-done((bf16[1,1,4,64,1024]{4,3,2,1,0:T(8,128)(2,1)S(1)}, bf16[1,1,4,64,1024]{4,3,2,1,0:T(8,128)(2,1)}, u32[]{:S(2)}) %copy-start) | copy-done | bytes 524312
  2.4 0.0 copy-start.1
  2.4 1.0 %copy-done.1 = bf16[1,1,4,64,1024]{4,3,2,1,0:T(8,128)(2,1)S(1)} copy-done((bf16[1,1,4,64,1024]{4,3,2,1,0:T(8,128)(2,1)S(1)}, bf16[1,1,4,64,1024]{4,3,2,1,0:T(8,128)(2,1)}, u32[]{:S(2)}) %copy-start.1) | copy-done | bytes 524312
  3.4 0.0 copy-start.2
  3.4 1.0 %copy-done.2 = bf16[1,1,4,64,1024]{4,3,2,1,0:T(8,128)(2,1)S(1)} copy-done((bf16[1,1,4,64,1024]{4,3,2,1,0:T(8,128)(2,1)S(1)}, bf16[1,1,4,64,1024]{4,3,2,1,0:T(8,128)(2,1)}, u32[]{:S(2)}) %copy-start.2) | copy-done | bytes 524312
  4.4 0.0 copy-start.3
  4.5 1.0 %copy-done.3 = bf16[1,1,4,64,1024]{4,3,2,1,0:T(8,128)(2,1)S(1)} copy-done((bf16[1,1,4,64,1024]{4,3,2,1,0:T(8,128)(2,1)S(1)}, bf16[1,1,4,64,1024]{4,3,2,1,0:T(8,128)(2,1)}, u32[]{:S(2)}) %copy-start.3) | copy-done | bytes 524312
  5.5 86.0 %shard_map.94 = (bf16[4,64,1024]{2,1,0:T(8,128)(2,1)S(1)}, bf16[4,64,1024]{2,1,0:T(8,128)(2,1)S(1)}, bf16[4,64,1024]{2,1,0:T(8,128)(2,1)S(1)}) custom-call(s32[4]{0:T(128)S(1)} %copy-done.5, s32[1,512]{1,0:T(1,128)S(1)} %copy-done.4, f32[1,8]{1,0:T(1,128)S(1)} %copy-done.6, bf16[4,64,1024]{2,1,0:T(8,128)(2,1)S(1)} %bitcast.7, ...), custom_call_target="tpu_custom_call" | custom-call | tf_op jit(solution)/shard_map/pallas_call | solution.py:384
  91.5 0.8 copy.13
  92.3 0.8 copy.14
  93.1 0.8 copy.15
Async XLA Ops:
  0.6 0.7 copy-start.4
  0.6 0.7 copy-start.5
  0.7 0.7 copy-start.6
  1.3 1.0 %copy-start = (bf16[1,1,4,64,1024]{4,3,2,1,0:T(8,128)(2,1)S(1)}, bf16[1,1,4,64,1024]{4,3,2,1,0:T(8,128)(2,1)}, u32[]{:S(2)}) copy-start(bf16[1,1,4,64,1024]{4,3,2,1,0:T(8,128)(2,1)} %param.7) | copy-start | bytes 1572868
  2.4 1.0 %copy-start.1 = (bf16[1,1,4,64,1024]{4,3,2,1,0:T(8,128)(2,1)S(1)}, bf16[1,1,4,64,1024]{4,3,2,1,0:T(8,128)(2,1)}, u32[]{:S(2)}) copy-start(bf16[1,1,4,64,1024]{4,3,2,1,0:T(8,128)(2,1)} %param.8) | copy-start | bytes 1572868
  3.4 1.0 %copy-start.2 = (bf16[1,1,4,64,1024]{4,3,2,1,0:T(8,128)(2,1)S(1)}, bf16[1,1,4,64,1024]{4,3,2,1,0:T(8,128)(2,1)}, u32[]{:S(2)}) copy-start(bf16[1,1,4,64,1024]{4,3,2,1,0:T(8,128)(2,1)} %param.9) | copy-start | bytes 1572868
  4.4 1.0 %copy-start.3 = (bf16[1,1,4,64,1024]{4,3,2,1,0:T(8,128)(2,1)S(1)}, bf16[1,1,4,64,1024]{4,3,2,1,0:T(8,128)(2,1)}, u32[]{:S(2)}) copy-start(bf16[1,1,4,64,1024]{4,3,2,1,0:T(8,128)(2,1)} %param.10) | copy-start | bytes 1572868

commit v2 on v1

--- a/solution.py
+++ b/solution.py
@@ -174,16 +174,14 @@
     k_ref,
     v_ref,
     d_ref,
-    dq_ref,
-    dk_ref,
-    dv_ref,
+    arrived_ref,
     *scratch,
 ):
-    (send, recv, back_send, loss_send, loss_recv, ids_row, weight) = scratch[:7]
-    back_recv = scratch[7 : 7 + heads_each]
-    send_sem, recv_sem, back_send_sem, back_recv_sem, loss_send_sem, loss_recv_sem = scratch[
-        7 + heads_each :
-    ]
+    send, recv, back_send, loss_send, loss_recv, ids_row, weight = scratch[:7]
+    loaded = scratch[7 : 7 + heads_each]
+    (load_sem, send_sem, recv_sem, back_send_sem, back_recv_sem, loss_send_sem, loss_recv_sem) = (
+        scratch[7 + heads_each :]
+    )
     z = lax.axis_index("dp")
     x = lax.axis_index("seq")
     me = z * n_seq + x
@@ -199,6 +197,22 @@
         pz, px = lax.rem(z + a, n_dp), lax.rem(x + b, n_seq)
         partners.append((pz, px, pz * n_seq + px))
 
+    def columns_of(s, c):
+        return pl.ds(pl.multiple_of((s * heads_each + c) * HD, HD), HD)
+
+    def loads(c):
+        return [
+            pltpu.make_async_copy(
+                ref.at[:, :, columns_of(s, c)], loaded[c].at[s, i], load_sem.at[c, s, i]
+            )
+            for s in range(n_seq)
+            for i, ref in enumerate((q_ref, k_ref, v_ref, d_ref))
+        ]
+
+    for c in range(heads_each):
+        for load in loads(c):
+            load.start()
+
     barrier = pltpu.get_barrier_semaphore()
     for pz, px, _ in partners:
         pl.semaphore_signal(
@@ -216,11 +230,12 @@
     taken = [group_with(lax.rem(n - z + n_dp, n_dp)) for n in range(n_dp)]
 
     def stage(c):
+        for load in loads(c):
+            load.wait()
         for n in range(n_dp):
             for s in range(n_seq):
-                cols = slice((s * heads_each + c) * HD, (s * heads_each + c + 1) * HD)
-                for i, ref in enumerate((q_ref, k_ref, v_ref, d_ref)):
-                    send[c, n * n_seq + s, i] = ref[taken[n], :, cols]
+                for i in range(4):
+                    send[c, n * n_seq + s, i] = loaded[c][s, i, taken[n]]
 
     def send_copy(c, pz, px, m):
         return pltpu.make_async_remote_copy(
@@ -245,17 +260,24 @@
     def back_copy(c, pz, px, m):
         return pltpu.make_async_remote_copy(
             src_ref=back_send.at[c, m],
-            dst_ref=back_recv[c].at[me],
+            dst_ref=arrived_ref.at[:, z, :, columns_of(x, c)],
             send_sem=back_send_sem.at[c, m],
             recv_sem=back_recv_sem.at[c, me],
             device_id={"dp": pz, "seq": px},
             device_id_type=MESH,
         )
 
+    def kept_copy(c):
+        return pltpu.make_async_copy(
+            back_send.at[c, me],
+            arrived_ref.at[:, z, :, columns_of(x, c)],
+            back_recv_sem.at[c, me],
+        )
+
     def back_arrival(c, pz, px, m):
         return pltpu.make_async_remote_copy(
             src_ref=back_send.at[c, m],
-            dst_ref=back_recv[c].at[m],
+            dst_ref=arrived_ref.at[:, pz, :, columns_of(px, c)],
             send_sem=back_send_sem.at[c, m],
             recv_sem=back_recv_sem.at[c, m],
             device_id={"dp": pz, "seq": px},
@@ -348,17 +370,12 @@
         work(c)
         for pz, px, m in partners:
             back_copy(c, pz, px, m).start()
-
-    packs = [lax.rem(z + offset[j], n_dp) for j in range(pieces)]
+        kept_copy(c).start()
+
     for c in range(heads_each):
-        back_recv[c][me] = back_send[c, me]
         for pz, px, m in partners:
             back_arrival(c, pz, px, m).wait_recv()
-        for s in range(n_seq):
-            cols = slice((s * heads_each + c) * HD, (s * heads_each + c + 1) * HD)
-            for j in range(pieces):
-                for i, ref in enumerate((dq_ref, dk_ref, dv_ref)):
-                    ref[j, :, cols] = back_recv[c][packs[j] * n_seq + s, i]
+        kept_copy(c).wait()
 
     for step in range(1, n_dp):
         loss_copy(step, True).wait_send()
@@ -366,6 +383,25 @@
         for pz, px, m in partners:
             send_copy(c, pz, px, m).wait_send()
             back_copy(c, pz, px, m).wait_send()
+
+
+def order_kernel(n_dp, pieces, offsets_ref, arrived_ref, dq_ref, dk_ref, dv_ref, held, in_sem, out_sem):
+    z = lax.axis_index("dp")
+    into, out = [], []
+    for j in range(pieces):
+        pack = lax.rem(z + offsets_ref[j], n_dp)
+        for i, ref in enumerate((dq_ref, dk_ref, dv_ref)):
+            into.append(
+                pltpu.make_async_copy(arrived_ref.at[i, pack], held.at[i, j], in_sem.at[i, j])
+            )
+            out.append(pltpu.make_async_copy(held.at[i, j], ref.at[j], out_sem.at[i, j]))
+    for copy in into:
+        copy.start()
+    for copy, after in zip(into, out):
+        copy.wait()
+        after.start()
+    for after in out:
+        after.wait()
 
 
 def kernel_shards(queries, key_vectors, value_rows, upstream, segments, losses, offsets):
@@ -381,11 +417,13 @@
     whole = pl.BlockSpec(memory_space=pltpu.VMEM)
     result = jax.ShapeDtypeStruct((pieces, rows, columns), jnp.bfloat16)
     dma = pltpu.SemaphoreType.DMA
-    grads = pl.pallas_call(
+    arrived = pl.pallas_call(
         functools.partial(exchange_kernel, n_dp, n_seq, pieces, rows, heads_each, images),
-        out_shape=(result,) * 3,
-        in_specs=[pl.BlockSpec(memory_space=pltpu.SMEM)] + [whole] * 6,
-        out_specs=(whole,) * 3,
+        out_shape=jax.ShapeDtypeStruct((3, n_dp, rows, columns), jnp.bfloat16),
+        in_specs=[pl.BlockSpec(memory_space=pltpu.SMEM)]
+        + [whole] * 2
+        + [pl.BlockSpec(memory_space=pl.ANY)] * 4,
+        out_specs=pl.BlockSpec(memory_space=pl.ANY),
         scratch_shapes=[
             pltpu.VMEM((heads_each, parts, 4, rows, HD), jnp.bfloat16),
             pltpu.VMEM((heads_each, parts, 4, rows, HD), jnp.bfloat16),
@@ -395,8 +433,9 @@
             pltpu.VMEM((8, parts * rows), jnp.float32),
             pltpu.VMEM((parts * rows, HD), jnp.float32),
         ]
-        + [pltpu.VMEM((parts, 3, rows, HD), jnp.bfloat16)] * heads_each
+        + [pltpu.VMEM((n_seq, 4, pieces, rows, HD), jnp.bfloat16)] * heads_each
         + [
+            dma((heads_each, n_seq, 4)),
             dma((heads_each, parts)),
             dma((heads_each, parts)),
             dma((heads_each, parts)),
@@ -405,9 +444,21 @@
             dma((n_dp,)),
         ],
         compiler_params=pltpu.CompilerParams(
-            collective_id=0, has_side_effects=True, vmem_limit_bytes=48 * 1024 * 1024
+            collective_id=0, has_side_effects=True, vmem_limit_bytes=56 * 1024 * 1024
         ),
     )(offsets, segments, losses, *arrays)
+    grads = pl.pallas_call(
+        functools.partial(order_kernel, n_dp, pieces),
+        out_shape=(result,) * 3,
+        in_specs=[pl.BlockSpec(memory_space=pltpu.SMEM), pl.BlockSpec(memory_space=pl.ANY)],
+        out_specs=(pl.BlockSpec(memory_space=pl.ANY),) * 3,
+        scratch_shapes=[
+            pltpu.VMEM((3, pieces, rows, columns), jnp.bfloat16),
+            dma((3, pieces)),
+            dma((3, pieces)),
+        ],
+        compiler_params=pltpu.CompilerParams(vmem_limit_bytes=56 * 1024 * 1024),
+    )(offsets, arrived)
     return tuple(g.reshape(1, 1, pieces, rows, columns) for g in grads)
 
 

time: 94.2 us -> 90.4 us (0.960)
  local copies, waits for them, and re-layouts: 7.21 us -> 0 us
  Pallas kernels: 86 us -> 89.5 us
    unnamed x17 -> x0, local copies, waits for them, and re-layouts: 7.21 us -> none
    pallas_call x0 -> x1, Pallas kernels: none -> 3.01 us  [kernel_shards(): pl.pallas_call(functools.partial(order_kernel, n_dp, pieces), out_shape=(...]
where the time goes in v2:
time: 90.4 us; the launch traced here: 90.1 us
  Pallas kernels  89.5 us (99%)
    pallas_call x1, Pallas kernels, kernel_shards(): pl.pallas_call(functools.partial(exchange_kernel, n_dp, n_seq, pieces, ro...  86.5 us
    pallas_call x1, Pallas kernels, kernel_shards(): pl.pallas_call(functools.partial(order_kernel, n_dp, pieces), out_shape=(...  3.01 us

profile of v2, /device:TPU:0, one launch (start us, length us, event | category | flops | bytes accessed | tf_op | source)
XLA Modules:
  0.0 90.1 jit_solution(10746569343551628006)
XLA Ops:
  0.6 86.5 %shard_map.94.arrived_ref = bf16[3,4,64,1024]{3,2,1,0:T(8,128)(2,1)} custom-call(s32[4]{0:T(128)} %offsets_ref.3, s32[1,512]{1,0:T(1,128)} %segments_ref.1, f32[1,8]{1,0:T(1,128)} %losses_ref.1, bf16[4,64,1024]{2,1,0:T(8,128)(2,1)} %bitcast.7, bf16[4,64,1024]{2,1,0:T(8,128)(2,1)} %bitcast.8, bf16[4,64,1024]{2,1,0:T(8,128)(2,1)} %bitcast.9, ...), custom_call_target="tpu_custom_call" | custom-call | tf_op jit(solution)/shard_map/pallas_call | solution.py:420
  87.1 3.0 %shard_map.95 = (bf16[4,64,1024]{2,1,0:T(8,128)(2,1)}, bf16[4,64,1024]{2,1,0:T(8,128)(2,1)}, bf16[4,64,1024]{2,1,0:T(8,128)(2,1)}) custom-call(s32[4]{0:T(128)} %offsets_ref.3, bf16[3,4,64,1024]{3,2,1,0:T(8,128)(2,1)} %shard_map.94.arrived_ref), custom_call_target="tpu_custom_call" | custom-call | tf_op jit(solution)/shard_map/pallas_call | solution.py:450
